TPU v7x, 256 devices: a whole 4x4x8 slice. The times are simulated.
256 devices in a mesh: pw: 32 (over z_lo, y, core), band: 8 (over x, z_hi).
Axes of the slice: x: 4, y: 4, z: 8 (z_hi: 2, z_lo: 4; z = z_hi * 4 + z_lo), core: 2. Of those that a mesh axis runs over, the one named last changes fastest.
Arguments:
- waves: bfloat16 [2, 40960, 7168], P(None, 'pw', 'band'), may hold values from -6 to 6
- projectors: bfloat16 [2, 128, 40960], P(None, 'band', 'pw'), may hold values from -0.01953125 to 0.01953125
- coupling: float32 [12, 13, 13], replicated, may hold values from -32.19938 to 32.19938
- offsets: int32 [12], replicated, may hold values from 0 to 119, as said below
- counts: int32 [12], replicated, may hold values from 9 to 13, as said below
Outputs:
- applied: bfloat16 [2, 40960, 7168], P(None, 'pw', 'band')
Inputs may be any that keep to these rules, and one draw needn't show every extreme that they name: `counts`: each atom has 9 or 13 projectors, exactly 5 atoms have 13, so the atoms fill all 128 projectors. offsets are the running sums of counts before each atom, so atoms take consecutive projectors in order.
All inputs are finite; a program needn't handle non-finite values.
Results may differ from a plain program's by a relative error of at most 0.0049.
Values may be sent and summed in bfloat16 or wider, within the bound.
No kernel may reach another device: no remote copies, remote signals or barrier semaphores. Data moves between devices by JAX's collectives and lax.ppermute only.
A program may use at most 64 MiB of HBM per device.

v0:
```python
import jax
import jax.numpy as jnp
from jax import lax
from jax.sharding import PartitionSpec as P

NP = 128
M = 13


def coupling_block(coupling, offsets, counts):
    proj = jnp.arange(NP, dtype=jnp.int32)
    local = jnp.arange(M, dtype=jnp.int32)
    target = offsets[:, None] + local[None, :]
    select = (proj[None, :, None] == target[:, None, :]) & (
        local[None, None, :] < counts[:, None, None]
    )
    select = select.astype(jnp.float32)
    sym = (coupling + jnp.swapaxes(coupling, 1, 2)) * 0.5
    return jnp.einsum("api,aij,aqj->pq", select, sym, select, precision=lax.Precision.HIGHEST)


def project(rows, waves):
    real = jnp.dot(rows[0], waves[0], preferred_element_type=jnp.float32) + jnp.dot(
        rows[1], waves[1], preferred_element_type=jnp.float32
    )
    imag = jnp.dot(rows[0], waves[1], preferred_element_type=jnp.float32) - jnp.dot(
        rows[1], waves[0], preferred_element_type=jnp.float32
    )
    return jnp.stack([real, imag])


def spread_back(rows, coupled):
    dims = (((0,), (0,)), ((), ()))
    real = lax.dot_general(
        rows[0], coupled[0], dims, preferred_element_type=jnp.float32
    ) - lax.dot_general(rows[1], coupled[1], dims, preferred_element_type=jnp.float32)
    imag = lax.dot_general(
        rows[0], coupled[1], dims, preferred_element_type=jnp.float32
    ) + lax.dot_general(rows[1], coupled[0], dims, preferred_element_type=jnp.float32)
    return jnp.stack([real, imag])


def shards(waves, projectors, coupling, offsets, counts):
    block = coupling_block(coupling, offsets, counts)
    gathered = lax.all_gather(projectors, "band", axis=1, tiled=True)
    partial_coeffs = project(gathered, waves)
    coeffs = lax.psum(partial_coeffs, "pw")
    coupled = jnp.einsum("pq,kqb->kpb", block, coeffs, precision=lax.Precision.HIGHEST).astype(
        jnp.bfloat16
    )
    result = spread_back(gathered, coupled)
    return result.astype(jnp.bfloat16)


def solution(mesh):
    placed = (P(None, "pw", "band"), P(None, "band", "pw"), P(), P(), P())
    return jax.shard_map(
        shards, mesh=mesh, in_specs=placed, out_specs=P(None, "pw", "band"), check_vma=False
    )
```

profile of v0, /device:TPU:2, one launch (start us, length us, event | category | flops | bytes accessed | tf_op | source)
XLA Modules:
  0.0 365.1 jit_solution(13705950301523723169)
XLA Ops:
  6.5 0.0 all-reduce.2.cloned.1.call-start
  6.5 0.0 copy-start.3
  6.5 54.1 %all_gather.3 = bf16[2,128,1280]{2,1,0:T(8,128)(2,1)S(1)} all-gather(bf16[2,16,1280]{2,1,0:T(8,128)(2,1)} %param.6), channel_id=1, replica_groups=mesh['pw'=32,'band'=8] {'band'}, dimensions={1}, use_global_device_ids=true | all-gather | bytes 737280 | tf_op jit(solution)/shard_map/all_gather | solution.py:45
  60.6 2.2 fusion.2
  62.8 2.2 fusion.4
  64.9 0.0 copy-done.3
  65.0 0.0 copy-start
  65.0 0.0 copy-start.1
  65.0 0.0 copy-start.2
  65.0 0.5 fusion.24
  65.5 0.5 fusion.18
  66.0 1.0 pad_maximum_fusion.1
  67.0 0.0 all-reduce.2.cloned.1.call-update
  67.0 0.0 copy-done
  67.1 0.2 copy.6
  67.2 0.0 copy-done.1
  67.2 0.1 iota_compare_fusion.1
  67.3 0.0 copy-done.2
  67.3 0.1 iota_add_fusion
  67.4 0.8 fusion.30
  68.1 0.8 fusion.28
  69.0 273.7 %all-reduce.2.cloned.1.call-done = f32[2,128,896]{2,1,0:T(8,128)} async-done(((f32[2,128,896]{2,1,0:T(8,128)}), f32[2,128,896]{2,1,0:T(8,128)}) %all-reduce.2.cloned.1.call-update) | async-done | bytes 917520 | tf_op jit(solution)/shard_map/psum | solution.py:47
  342.7 2.8 fusion.14
  345.5 0.7 fusion.36
  346.2 0.7 fusion.37
  347.0 0.8 fusion.1
  347.7 0.8 fusion
  348.5 2.5 pad_maximum_fusion
  350.9 7.3 %copy.8 = bf16[2,1280,896]{2,1,0:T(8,128)(2,1)} copy(bf16[2,1280,896]{1,2,0:T(8,128)(2,1)} %pad_maximum_fusion) | data formatting | bytes 9175040 | tf_op jit(solution)/shard_map/stack | solution.py:40
Async XLA Ops:
  6.5 336.2 %all-reduce.2.cloned.1.call-start = ((), (), s32[]{:S(2)}) async-start(), calls=%async_computation | async-start | bytes 1835008 | tf_op jit(solution)/shard_map/psum | solution.py:47
  6.5 58.4 %copy-start.3 = (bf16[2,1280,896]{2,1,0:T(8,128)(2,1)S(1)}, bf16[2,1280,896]{2,1,0:T(8,128)(2,1)}, u32[]{:S(2)}) copy-start(bf16[2,1280,896]{2,1,0:T(8,128)(2,1)} %param.5) | copy-start | bytes 13762564
  65.0 2.1 copy-start
  65.0 2.2 copy-start.1
  65.0 2.3 copy-start.2
Sparse Core Ops, SparseCore 0:
  67.2 275.4 all-reduce.1
where the time goes:
time: 365 us
  waiting for transfers between devices  274 us (75%)
  blocking collectives  54.1 us (15%)
  between operations  13.5 us (4%)
  matrix products  12.7 us (3%)
  local copies, waits for them, and re-layouts  7.46 us (2%)
    psum x1, waiting for transfers between devices, shards(): coeffs = lax.psum(partial_coeffs, 'pw')  274 us
    all_gather x1, blocking collectives, shards(): gathered = lax.all_gather(projectors, 'band', axis=1, tiled=True)  54.1 us
  transfers between devices with their start and end apart: 1, of which 1 were waited for; matrix products, arithmetic and copies ran while one was open for 1% of the time, Pallas kernels for 0%

commit v1 on v0

--- a/solution.py
+++ b/solution.py
@@ -44,7 +44,7 @@
     block = coupling_block(coupling, offsets, counts)
     gathered = lax.all_gather(projectors, "band", axis=1, tiled=True)
     partial_coeffs = project(gathered, waves)
-    coeffs = lax.psum(partial_coeffs, "pw")
+    coeffs = jnp.sum(lax.all_gather(partial_coeffs, "pw"), axis=0)
     coupled = jnp.einsum("pq,kqb->kpb", block, coeffs, precision=lax.Precision.HIGHEST).astype(
         jnp.bfloat16
     )

time: 365 us -> 266 us (0.73)
  waiting for transfers between devices: 274 us -> 164 us
  other arithmetic: 3.59 us -> 14.1 us
    psum x1 -> x0, waiting for transfers between devices: 274 us -> none  [shards(): coeffs = lax.psum(partial_coeffs, 'pw')]
    all_gather x0 -> x1, waiting for transfers between devices: none -> 164 us  [shards(): coeffs = jnp.sum(lax.all_gather(partial_coeffs, 'pw'), axis=0)]
    reduce_sum x0 -> x1, other arithmetic: none -> 10.5 us  [shards(): coeffs = jnp.sum(lax.all_gather(partial_coeffs, 'pw'), axis=0)]
where the time goes in v1:
time: 266 us; the launch traced here: 265 us
  waiting for transfers between devices  164 us (62%)
  blocking collectives  54.1 us (20%)
  other arithmetic  14.1 us (5%)
  between operations  13.5 us (5%)
  matrix products  11.5 us (4%)
  local copies, waits for them, and re-layouts  7.46 us (3%)
    all_gather x1, waiting for transfers between devices, shards(): coeffs = jnp.sum(lax.all_gather(partial_coeffs, 'pw'), axis=0)  164 us
    all_gather x1, blocking collectives, shards(): gathered = lax.all_gather(projectors, 'band', axis=1, tiled=True)  54.1 us
    reduce_sum x1, other arithmetic, shards(): coeffs = jnp.sum(lax.all_gather(partial_coeffs, 'pw'), axis=0)  10.5 us
    another operation x1, local copies, waits for them, and re-layouts, spread_back(): return jnp.stack([real, imag])  7.27 us
  transfers between devices with their start and end apart: 1, of which 1 were waited for; matrix products, arithmetic and copies ran while one was open for 1% of the time, Pallas kernels for 0%

profile of v1, /device:TPU:2, one launch (start us, length us, event | category | flops | bytes accessed | tf_op | source)
XLA Modules:
  0.0 264.8 jit_solution(17942068290631853248)
XLA Ops:
  6.5 0.0 all-gather.3.cloned.1.call-start
  6.5 0.0 copy-start.3
  6.5 54.1 %all_gather.9 = bf16[2,128,1280]{2,1,0:T(8,128)(2,1)S(1)} all-gather(bf16[2,16,1280]{2,1,0:T(8,128)(2,1)} %param.6), channel_id=1, replica_groups=mesh['pw'=32,'band'=8] {'band'}, dimensions={1}, use_global_device_ids=true | all-gather | bytes 737280 | tf_op jit(solution)/shard_map/all_gather | solution.py:45
  60.6 2.2 fusion.4
  62.8 2.2 fusion.2
  64.9 0.0 copy-done.3
  65.0 0.0 copy-start
  65.0 0.0 copy-start.1
  65.0 0.0 copy-start.2
  65.0 0.5 fusion.18
  65.5 0.5 fusion.24
  66.0 1.0 pad_maximum_fusion.1
  67.0 0.0 all-gather.3.cloned.1.call-update
  67.0 0.0 copy-done
  67.1 0.2 copy.8
  67.2 0.0 copy-done.1
  67.2 0.1 iota_compare_fusion.1
  67.3 0.0 copy-done.2
  67.3 0.1 iota_add_fusion
  67.4 0.8 fusion.30
  68.1 0.8 fusion.28
  69.0 164.2 %all-gather.3.cloned.1.call-done = f32[64,128,896]{2,1,0:T(8,128)} async-done(((f32[2,128,896]{2,1,0:T(8,128)}), f32[64,128,896]{2,1,0:T(8,128)}) %all-gather.3.cloned.1.call-update) | async-done | bytes 29360144 | tf_op jit(solution)/shard_map/all_gather | solution.py:47
  233.1 10.5 %reduce_sum.9 = f32[2,128,896]{2,1,0:T(8,128)S(1)} reduce(f32[32,2,128,896]{3,2,1,0:T(8,128)} %bitcast.62, f32[]{:T(128)} %constant.0.clone.1), dimensions={0}, to_apply=%region_0.0 | reduce | flops 7110656 | bytes 30277636 | tf_op jit(solution)/shard_map/reduce_sum | solution.py:47
  243.6 1.6 fusion.14
  245.2 0.7 fusion.37
  246.0 0.7 fusion.36
  246.7 0.8 fusion
  247.5 0.8 fusion.1
  248.2 2.5 pad_maximum_fusion
  250.7 7.3 %copy.10 = bf16[2,1280,896]{2,1,0:T(8,128)(2,1)} copy(bf16[2,1280,896]{1,2,0:T(8,128)(2,1)} %pad_maximum_fusion) | data formatting | bytes 9175040 | tf_op jit(solution)/shard_map/stack | solution.py:40
Async XLA Ops:
  6.5 226.6 %all-gather.3.cloned.1.call-start = ((), (), s32[]{:S(2)}) async-start(), calls=%async_computation | async-start | bytes 30277632 | tf_op jit(solution)/shard_map/all_gather | solution.py:47
  6.5 58.4 %copy-start.3 = (bf16[2,1280,896]{2,1,0:T(8,128)(2,1)S(1)}, bf16[2,1280,896]{2,1,0:T(8,128)(2,1)}, u32[]{:S(2)}) copy-start(bf16[2,1280,896]{2,1,0:T(8,128)(2,1)} %param.5) | copy-start | bytes 13762564
  65.0 2.1 copy-start
  65.0 2.2 copy-start.1
  65.0 2.3 copy-start.2
Sparse Core Ops, SparseCore 0:
  67.2 165.9 all-gather.2

commit v2 on v0

--- a/solution.py
+++ b/solution.py
@@ -42,7 +42,9 @@
 
 def shards(waves, projectors, coupling, offsets, counts):
     block = coupling_block(coupling, offsets, counts)
-    gathered = lax.all_gather(projectors, "band", axis=1, tiled=True)
+    gathered = jnp.concatenate(
+        lax.all_to_all(jnp.stack([projectors] * lax.axis_size("band")), "band", 0, 0), axis=1
+    )
     partial_coeffs = project(gathered, waves)
     coeffs = lax.psum(partial_coeffs, "pw")
     coupled = jnp.einsum("pq,kqb->kpb", block, coeffs, precision=lax.Precision.HIGHEST).astype(

time: 365 us -> 336 us (0.921)
  blocking collectives: 54.1 us -> 30.2 us
  waiting for transfers between devices: 274 us -> 269 us
    all_gather x1 -> x0, blocking collectives: 54.1 us -> none  [shards(): gathered = lax.all_gather(projectors, 'band', axis=1, tiled=True)]
    all_to_all x0 -> x1, blocking collectives: none -> 30.2 us  [shards(): lax.all_to_all(jnp.stack([projectors] * lax.axis_size('band')), 'band', 0...]
    psum x1, waiting for transfers between devices: 274 us -> 269 us  [shards(): coeffs = lax.psum(partial_coeffs, 'pw')]
where the time goes in v2:
time: 336 us
  waiting for transfers between devices  269 us (80%)
  blocking collectives  30.2 us (9%)
  between operations  13.5 us (4%)
  matrix products  11.1 us (3%)
  local copies, waits for them, and re-layouts  8.58 us (3%)
  other arithmetic  3.6 us (1%)
    psum x1, waiting for transfers between devices, shards(): coeffs = lax.psum(partial_coeffs, 'pw')  269 us
    all_to_all x1, blocking collectives, shards(): lax.all_to_all(jnp.stack([projectors] * lax.axis_size('band')), 'band', 0...  30.2 us
    another operation x1, local copies, waits for them, and re-layouts, spread_back(): return jnp.stack([real, imag])  7.27 us
  transfers between devices with their start and end apart: 1, of which 1 were waited for; matrix products, arithmetic and copies ran while one was open for 1% of the time, Pallas kernels for 0%

profile of v2, /device:TPU:2, one launch (start us, length us, event | category | flops | bytes accessed | tf_op | source)
XLA Modules:
  0.0 336.0 jit_solution(3935263034095764991)
XLA Ops:
  6.5 0.0 all-reduce.2.cloned.1.call-start
  6.5 0.0 copy-start
  6.5 1.1 stack.32
  7.6 30.2 %all_to_all.5 = bf16[8,2,16,1280]{3,2,1,0:T(8,128)(2,1)S(1)} all-to-all(bf16[8,2,16,1280]{3,2,1,0:T(8,128)(2,1)S(1)} %stack.32), channel_id=1, replica_groups=mesh['pw'=32,'band'=8] {'band'}, dimensions={0} | all-to-all | bytes 1310720 | tf_op jit(solution)/shard_map/all_to_all | solution.py:46
  37.9 2.2 fusion.2
  40.1 0.0 copy-done
  40.1 0.5 fusion.4
  40.6 0.0 copy-start.1
  40.6 0.0 copy-start.2
  40.6 0.0 copy-start.3
  40.6 0.5 fusion.24
  41.2 0.5 fusion.18
  41.7 1.0 pad_maximum_fusion.1
  42.7 0.0 all-reduce.2.cloned.1.call-update
  42.7 0.0 copy-done.1
  42.7 0.2 copy.6
  42.9 0.0 copy-done.2
  42.9 0.1 iota_compare_fusion.1
  42.9 0.0 copy-done.3
  42.9 0.1 iota_add_fusion
  43.0 0.8 fusion.30
  43.8 0.8 fusion.28
  44.6 269.0 %all-reduce.2.cloned.1.call-done = f32[2,128,896]{2,1,0:T(8,128)} async-done(((f32[2,128,896]{2,1,0:T(8,128)}), f32[2,128,896]{2,1,0:T(8,128)}) %all-reduce.2.cloned.1.call-update) | async-done | bytes 917520 | tf_op jit(solution)/shard_map/psum | solution.py:49
  313.6 2.8 fusion.14
  316.4 0.7 fusion.37
  317.2 0.7 fusion.36
  317.9 0.8 fusion.1
  318.7 0.8 fusion
  319.4 2.5 pad_maximum_fusion
  321.9 7.3 %copy.8 = bf16[2,1280,896]{2,1,0:T(8,128)(2,1)} copy(bf16[2,1280,896]{1,2,0:T(8,128)(2,1)} %pad_maximum_fusion) | data formatting | bytes 9175040 | tf_op jit(solution)/shard_map/stack | solution.py:40
  (1 shorter events, 0.0 us)
Async XLA Ops:
  6.5 307.1 %all-reduce.2.cloned.1.call-start = ((), (), s32[]{:S(2)}) async-start(), calls=%async_computation.1 | async-start | bytes 1835008 | tf_op jit(solution)/shard_map/psum | solution.py:49
  6.5 33.5 %copy-start = (bf16[2,1280,896]{2,1,0:T(8,128)(2,1)S(1)}, bf16[2,1280,896]{2,1,0:T(8,128)(2,1)}, u32[]{:S(2)}) copy-start(bf16[2,1280,896]{2,1,0:T(8,128)(2,1)} %param.5) | copy-start | bytes 13762564
  40.6 2.1 copy-start.1
  40.6 2.2 copy-start.2
  40.6 2.3 copy-start.3
Sparse Core Ops, SparseCore 0:
  42.8 270.7 all-reduce.1
